TPU v7x, 32 devices: a whole 2x2x4 slice. The times are simulated.
32 devices in a mesh: groups: 2 (over x), inp: 16 (over z, y, core).
Axes of the slice: x: 2, y: 2, z: 4, core: 2. Of those that a mesh axis runs over, the one named last changes fastest.
Arguments:
- tokens: bfloat16 [512, 6144], P(('groups', 'inp')), parts along dimension 0, may hold values from -6 to 6
- dropout_masks: int32 [8, 512, 48], P(None, 'groups'), parts along dimension 1, may hold values 0 or 1
- input_gain: float32 [6144], replicated, may hold values from 0.5 to 1.5
- w_qkv: bfloat16 [128, 3, 48, 6144], P('inp'), may hold values from -0.078125 to 0.078125
- w_up: bfloat16 [24576, 6144], P('inp'), may hold values from -0.078125 to 0.078125
- query_gain: float32 [128], replicated, may hold values from 0.1 to 1.9
- key_gain: float32 [128], replicated, may hold values from 0.1 to 1.9
- w_proj: bfloat16 [128, 48, 6144], P('inp'), may hold values from -0.109375 to 0.109375
- w_down: bfloat16 [24576, 6144], P('inp'), may hold values from -0.0546875 to 0.0546875
- final_gain: float32 [6144], replicated, may hold values from 0.5 to 1.5
- w_head: bfloat16 [6144, 1000], P('inp'), may hold values from -0.625 to 0.625
Outputs:
- embedding: float32 [2, 8, 6144], P('groups', None, 'inp'), parts along dimension 0
- bald: float32 [2], P('groups'), parts along dimension 0
There are 2 independent parts, one for each index of `groups`. A program takes and returns all parts, laid end to end along the dimension named above; an argument that names none is the same for every part. Nothing has to cross between parts.
All inputs are finite; a program needn't handle non-finite values.
Results may differ from a plain program's by a relative error of at most 0.0093.
Values may be sent and summed in bfloat16 or wider, within the bound.
No kernel may reach another device: no remote copies, remote signals or barrier semaphores. Data moves between devices by JAX's collectives and lax.ppermute only.
A program may use at most 256 MiB of HBM per device.

v0:
```python
import math

import jax
import jax.numpy as jnp
from jax import lax
from jax.sharding import PartitionSpec as P

PATCHES = 256


soft_cap = 20.0


def norm_last(values, gain):
    average = jnp.mean(values, axis=-1, keepdims=True)
    centered = values - average
    spread_sq = jnp.mean(centered * centered, axis=-1, keepdims=True)
    return centered * lax.rsqrt(spread_sq + 1e-06) * gain


def norm_second(values, gain):
    average = jnp.mean(values, axis=1, keepdims=True)
    centered = values - average
    spread_sq = jnp.mean(centered * centered, axis=1, keepdims=True)
    return centered * lax.rsqrt(spread_sq + 1e-06) * gain[None, :, None, None]


def bald_score(logits):
    exp_logits = jnp.exp(logits)
    totals = jnp.sum(exp_logits, axis=-1, keepdims=True)
    sample_probs = exp_logits / totals
    entropy = jnp.log(totals[..., 0]) - jnp.sum(sample_probs * logits, axis=-1)
    mean_probs = jnp.mean(sample_probs, axis=1)
    joint = -jnp.sum(mean_probs * jnp.log(mean_probs), axis=-1)
    return joint - jnp.mean(entropy, axis=1)


def local(
    tokens,
    dropout_masks,
    input_gain,
    w_qkv,
    w_up,
    query_gain,
    key_gain,
    w_proj,
    w_down,
    final_gain,
    w_head,
):
    n_parts = lax.axis_size("inp")
    local_rows, model_width = tokens.shape
    n_masks, all_rows, n_blocks = dropout_masks.shape
    block_width = model_width // n_blocks
    n_comps, three_kinds, n_heads, ignored_width = w_qkv.shape
    n_units = w_up.shape[0]
    head_dim = n_comps * n_parts
    images = all_rows // PATCHES
    qkv_cols = three_kinds * n_heads * n_comps
    items_dev = n_masks * n_heads // n_parts
    highest = lax.Precision.HIGHEST
    joined_weight = jnp.concatenate(
        [jnp.transpose(w_qkv, (1, 2, 0, 3)).reshape(qkv_cols, model_width), w_up], axis=0
    )
    row_piece = lax.all_gather(tokens, "inp", axis=0, tiled=True)
    row_count = row_piece.shape[0]
    normed = norm_last(row_piece.astype(jnp.float32), input_gain).astype(jnp.bfloat16)
    masked = (
        normed.reshape(1, row_count, n_blocks, block_width)
        * dropout_masks.astype(jnp.bfloat16)[..., None]
    )
    masked = masked.reshape(n_masks, row_count, model_width)
    result = jnp.einsum("mkd,cd->mck", masked, joined_weight, preferred_element_type=jnp.float32)
    projected = 2.0 * result
    qkv_half = (
        projected[:, :qkv_cols]
        .astype(jnp.bfloat16)
        .reshape(n_masks, three_kinds, n_heads * n_comps, all_rows)
    )
    item_shape = (n_parts, items_dev, n_comps, all_rows)
    query_send = qkv_half[:, 0].reshape(item_shape)
    key_send = qkv_half[:, 1].reshape(item_shape)
    value_send = qkv_half[:, 2].reshape(item_shape)
    activated = jax.nn.gelu(projected[:, qkv_cols:], approximate=False)
    pooled_hidden = jnp.mean(activated.reshape(n_masks, n_units, images, PATCHES), axis=-1).astype(
        jnp.bfloat16
    )
    query_in = lax.all_to_all(query_send, "inp", split_axis=0, concat_axis=2, tiled=True)
    key_in = lax.all_to_all(key_send, "inp", split_axis=0, concat_axis=2, tiled=True)
    value_in = lax.all_to_all(value_send, "inp", split_axis=0, concat_axis=2, tiled=True)
    n_items = query_in.shape[1]
    shape_four = (n_items, head_dim, images, PATCHES)
    query_norm = norm_second(query_in.reshape(shape_four).astype(jnp.float32), query_gain).astype(
        jnp.bfloat16
    )
    key_norm = norm_second(key_in.reshape(shape_four).astype(jnp.float32), key_gain).astype(
        jnp.bfloat16
    )
    scores = jnp.einsum(
        "jcip,jciq->jipq", query_norm, key_norm, preferred_element_type=jnp.float32
    ) / math.sqrt(head_dim)
    exp_scores = jnp.exp(scores)
    weights = (exp_scores / jnp.sum(exp_scores, axis=-1, keepdims=True)).astype(jnp.bfloat16)
    query_mean = jnp.sum(weights, axis=2, dtype=jnp.float32) / PATCHES
    pooled = jnp.einsum(
        "jiq,jciq->jic",
        query_mean,
        value_in.reshape(shape_four).astype(jnp.float32),
        precision=highest,
    )
    attended = pooled.astype(jnp.bfloat16)[None]
    returned = lax.all_to_all(attended, "inp", split_axis=3, concat_axis=0, tiled=True)
    returned = returned.reshape(n_masks, n_heads, images, n_comps)
    mixed_sum = jnp.einsum("mhic,chd->imd", returned, w_proj, preferred_element_type=jnp.float32)
    mixed_sum = mixed_sum + jnp.einsum(
        "mfi,fd->imd", pooled_hidden, w_down, preferred_element_type=jnp.float32
    )
    row_ids = lax.axis_index("inp") * local_rows + jnp.arange(local_rows, dtype=jnp.int32)
    row_owner = (row_ids // PATCHES)[None, :] == jnp.arange(images, dtype=jnp.int32)[:, None]
    input_sum = (
        jnp.dot(row_owner.astype(jnp.bfloat16), tokens, preferred_element_type=jnp.float32)
        / PATCHES
    )
    partial_feature = mixed_sum + input_sum[:, None, :]
    feature = lax.psum(partial_feature, "inp")
    normalized = norm_last(feature, final_gain)
    slice_width = model_width // n_parts
    embedding = lax.dynamic_slice_in_dim(
        normalized, lax.axis_index("inp") * slice_width, slice_width, 2
    )
    logit_part = jnp.einsum(
        "imd,dc->imc", embedding.astype(jnp.bfloat16), w_head, preferred_element_type=jnp.float32
    )
    raw_logits = lax.psum(logit_part, "inp")
    logits = soft_cap * jnp.tanh(raw_logits / soft_cap)
    return (embedding, bald_score(logits))


def solution(mesh):
    return jax.shard_map(
        local,
        mesh=mesh,
        in_specs=(
            P(("groups", "inp"), None),
            P(None, "groups", None),
            P(),
            P("inp", None, None, None),
            P("inp", None),
            P(),
            P(),
            P("inp", None, None),
            P("inp", None),
            P(),
            P("inp", None),
        ),
        out_specs=(P("groups", None, "inp"), P("groups")),
        check_vma=False,
    )
```

profile of v0, /device:TPU:0, one launch (start us, length us, event | category | flops | bytes accessed | tf_op | source)
XLA Modules:
  0.0 515.5 jit_solution(8869411747633825082)
XLA Ops:
  7.2 0.0 copy-start
  7.2 0.0 all-gather.2.cloned.1.call-start
  7.2 0.7 all-gather.2.cloned.1.call-update
  7.9 1.0 convert_element_type.93
  8.9 0.3 copy.40
  9.2 16.1 %mul.160 = bf16[8,256,48,128]{3,2,1,0:T(8,128)(2,1)} broadcast(bf16[8,256,48]{2,1,0:T(8,128)(2,1)S(1)} %copy.40), dimensions={0,1,2} | broadcast | bytes 25362432 | tf_op jit(solution)/shard_map/mul | solution.py:69
  25.4 35.7 %mul.161 = bf16[8,256,6144]{2,1,0:T(8,128)(2,1)} reshape(bf16[8,256,48,128]{3,2,1,0:T(8,128)(2,1)} %mul.160) | data formatting | bytes 50331648 | tf_op jit(solution)/shard_map/mul | solution.py:69
  61.1 0.0 copy-start.3
  61.1 15.2 %copy.39 = bf16[3,48,8,6144]{3,2,1,0:T(8,128)(2,1)} copy(bf16[3,48,8,6144]{3,1,0,2:T(8,128)(2,1)} %bitcast.130) | data formatting | bytes 28311552 | tf_op jit(solution)/shard_map/transpose | solution.py:63
  76.3 0.0 all-gather.2.cloned.1.call-done
  76.3 2.4 convert_reduce_fusion
  78.7 2.9 fusion.23
  81.5 0.0 copy-done.3
  81.5 4.8 fusion.25
  86.3 82.9 %multiply_bitcast_fusion = f32[8,2688,256]{2,1,0:T(8,128)} fusion(bf16[8,256,6144]{2,1,0:T(8,128)(2,1)} %mul.161, bf16[1536,6144]{1,0:T(8,128)(2,1)} %param.15, bf16[1152,6144]{1,0:T(8,128)(2,1)} %bitcast.131, bf16[256,6144]{1,0:T(8,128)(2,1)} %fusion.25), kind=kOutput, calls=%fused_computation.6 | convolution fusion | flops 67767631872 | bytes 83361792 | tf_op jit(solution)/shard_map/mkd,cd->mck/dot_general | solution.py:73
  169.2 0.0 copy-start.1
  169.2 4.2 slice.28
  173.5 0.0 copy-start.4
  173.5 0.0 copy-start.5
  173.5 2.0 fusion.83
  175.5 43.2 %all_to_all.48 = bf16[16,24,8,256]{3,2,1,0:T(8,128)(2,1)S(1)} all-to-all(bf16[16,24,8,256]{3,2,1,0:T(8,128)(2,1)S(1)} %bitcast.134), channel_id=1, replica_groups=mesh['groups'=2,'inp'=16] {'inp'}, dimensions={0} | all-to-all | bytes 3145728 | tf_op jit(solution)/shard_map/all_to_all | solution.py:88
  218.7 5.1 all-to-all-start.1
  223.8 0.0 copy-done.1
  223.8 0.2 fusion.61
  223.9 0.3 fusion.41
  224.2 31.6 %all-to-all-done.1 = bf16[16,24,8,256]{3,2,1,0:T(8,128)(2,1)} async-done(((bf16[16,24,8,256]{3,2,1,0:T(8,128)(2,1)}), bf16[16,24,8,256]{3,2,1,0:T(8,128)(2,1)}, u32[]{:S(2)}, u32[]{:S(2)}) %all-to-all-start.1) | async-done | bytes 1572896 | tf_op jit(solution)/shard_map/all_to_all | solution.py:89
  255.8 9.2 %all-to-all-start.2 = ((bf16[16,24,8,256]{3,2,1,0:T(8,128)(2,1)}), bf16[16,24,8,256]{3,2,1,0:T(8,128)(2,1)}, u32[]{:S(2)}, u32[]{:S(2)}) async-start(bf16[16,24,8,256]{3,2,1,0:T(8,128)(2,1)} %bitcast.132), calls=%async_computation.2 | async-start | bytes 3145728 | tf_op jit(solution)/shard_map/all_to_all | solution.py:90
  265.0 1.7 fusion.27
  266.6 0.5 multiply_reduce_fusion
  267.1 1.9 fusion.30
  269.0 0.0 copy-done.4
  269.0 0.0 copy-done.5
  269.0 2.8 fusion.39
  271.8 2.1 convert_reduce_fusion.1
  273.9 23.1 %all-to-all-done.2 = bf16[16,24,8,256]{3,2,1,0:T(8,128)(2,1)} async-done(((bf16[16,24,8,256]{3,2,1,0:T(8,128)(2,1)}), bf16[16,24,8,256]{3,2,1,0:T(8,128)(2,1)}, u32[]{:S(2)}, u32[]{:S(2)}) %all-to-all-start.2) | async-done | bytes 1572896 | tf_op jit(solution)/shard_map/all_to_all | solution.py:90
  297.0 2.7 fusion.43
  299.7 0.8 copy.47
  300.5 9.1 %all-to-all-start.3 = ((bf16[1,24,1,128]{1,2,0,3:T(2,128)(2,1)}), bf16[1,24,1,128]{1,2,0,3:T(2,128)(2,1)S(1)}, u32[]{:S(2)}, u32[]{:S(2)}) async-start(bf16[1,24,1,128]{1,2,0,3:T(2,128)(2,1)} %copy.47), calls=%async_computation.3 | async-start | bytes 131072 | tf_op jit(solution)/shard_map/all_to_all | solution.py:112
  309.6 0.0 all-reduce.2.cloned.1.call-start
  309.7 29.6 %fusion.9 = f32[8,1536]{1,0:T(8,128)S(1)} fusion(f32[8,2688,256]{2,1,0:T(8,128)} %multiply_bitcast_fusion), kind=kLoop, calls=%fused_computation.10 | loop fusion | flops 204460032 | bytes 12632064 | tf_op jit(solution)/shard_map/reduce_sum | solution.py:85
  339.3 0.0 all-to-all-done.3
  339.3 0.1 reshape.233
  339.4 3.1 convolution_bitcast_fusion
  342.5 9.6 %fusion.22 = f32[1,8,6144]{2,1,0:T(8,128)} fusion(f32[8,6144]{1,0:T(8,128)S(1)} %convolution_bitcast_fusion, bf16[1536,6144]{1,0:T(8,128)(2,1)} %param.19, f32[6144]{0:T(1024)S(1)} %broadcast_multiply_fusion, f32[8,1536]{1,0:T(8,128)S(1)} %fusion.9), kind=kOutput, calls=%fused_computation.35 | convolution fusion | flops 151117824 | bytes 19341312 | tf_op jit(solution)/shard_map/mfi,fd->imd/dot_general | solution.py:115
  352.1 0.0 all-reduce.2.cloned.1.call-update
  352.2 0.8 dynamic-slice
  353.0 90.4 %all-reduce.2.cloned.1.call-done = f32[1,8,6144]{2,1,0:T(8,128)} async-done(((f32[1,8,6144]{2,1,0:T(8,128)}), f32[1,8,6144]{2,1,0:T(8,128)}) %all-reduce.2.cloned.1.call-update) | async-done | bytes 196624 | tf_op jit(solution)/shard_map/psum | solution.py:125
  443.4 1.1 reduce_sum.153
  444.5 1.2 multiply_reduce_fusion.1
  445.6 0.1 fusion.57
  445.7 0.0 copy-done
  445.7 0.0 copy-start.2
  445.7 0.3 convolution_bitcast_fusion.1
  446.0 58.5 %psum.15 = f32[1,8,1000]{2,1,0:T(8,128)S(1)} all-reduce(f32[1,8,1000]{2,1,0:T(8,128)S(1)} %convolution_bitcast_fusion.1), channel_id=1, replica_groups=mesh['groups'=2,'inp'=16] {'inp'}, use_global_device_ids=true, to_apply=%region_12.13 | all-reduce | flops 8000 | bytes 64000 | tf_op jit(solution)/shard_map/psum | solution.py:134
  504.6 0.1 exponential_reduce_fusion
  504.7 0.2 multiply_reduce_fusion.2
  504.9 0.7 subtract_reduce_fusion
  505.6 0.6 fusion.60
  507.5 0.0 copy-done.2
  (13 shorter events, 0.1 us)
Async XLA Ops:
  7.2 438.5 %copy-start = (bf16[384,1000]{0,1:T(8,128)(2,1)S(1)}, bf16[384,1000]{0,1:T(8,128)(2,1)}, u32[]{:S(2)}) copy-start(bf16[384,1000]{0,1:T(8,128)(2,1)} %param.21) | copy-start | bytes 2304004
  7.2 69.1 %all-gather.2.cloned.1.call-start = ((), (), s32[]{:S(2)}) async-start(), calls=%async_computation.4 | async-start | bytes 3342336 | tf_op jit(solution)/shard_map/all_gather | solution.py:65
  61.1 20.5 %copy-start.3 = (f32[6144]{0:T(1024)S(1)}, f32[6144]{0:T(1024)}, u32[]{:S(2)}) copy-start(f32[6144]{0:T(1024)} %param.13) | copy-start | bytes 73732
  169.2 54.5 %copy-start.1 = (bf16[16,6144]{1,0:T(8,128)(2,1)S(1)}, bf16[16,6144]{1,0:T(8,128)(2,1)}, u32[]{:S(2)}) copy-start(bf16[16,6144]{1,0:T(8,128)(2,1)} %param.11) | copy-start | bytes 589828
  173.5 95.5 %copy-start.4 = (f32[128]{0:T(128)S(1)}, f32[128]{0:T(128)}, u32[]{:S(2)}) copy-start(f32[128]{0:T(128)} %param.17) | copy-start | bytes 1540
  173.5 95.5 %copy-start.5 = (f32[128]{0:T(128)S(1)}, f32[128]{0:T(128)}, u32[]{:S(2)}) copy-start(f32[128]{0:T(128)} %param.16) | copy-start | bytes 1540
  218.7 37.1 %all-to-all-start.1 = ((bf16[16,24,8,256]{3,2,1,0:T(8,128)(2,1)}), bf16[16,24,8,256]{3,2,1,0:T(8,128)(2,1)}, u32[]{:S(2)}, u32[]{:S(2)}) async-start(bf16[16,24,8,256]{3,2,1,0:T(8,128)(2,1)} %bitcast.133), calls=%async_computation.1 | async-start | bytes 3145728 | tf_op jit(solution)/shard_map/all_to_all | solution.py:89
  255.8 41.2 %all-to-all-start.2 = ((bf16[16,24,8,256]{3,2,1,0:T(8,128)(2,1)}), bf16[16,24,8,256]{3,2,1,0:T(8,128)(2,1)}, u32[]{:S(2)}, u32[]{:S(2)}) async-start(bf16[16,24,8,256]{3,2,1,0:T(8,128)(2,1)} %bitcast.132), calls=%async_computation.2 | async-start | bytes 3145728 | tf_op jit(solution)/shard_map/all_to_all | solution.py:90
  300.5 38.8 %all-to-all-start.3 = ((bf16[1,24,1,128]{1,2,0,3:T(2,128)(2,1)}), bf16[1,24,1,128]{1,2,0,3:T(2,128)(2,1)S(1)}, u32[]{:S(2)}, u32[]{:S(2)}) async-start(bf16[1,24,1,128]{1,2,0,3:T(2,128)(2,1)} %copy.47), calls=%async_computation.3 | async-start | bytes 131072 | tf_op jit(solution)/shard_map/all_to_all | solution.py:112
  309.6 133.8 %all-reduce.2.cloned.1.call-start = ((), (), s32[]{:S(2)}) async-start(), calls=%async_computation.5 | async-start | bytes 393216 | tf_op jit(solution)/shard_map/psum | solution.py:125
  445.7 61.8 %copy-start.2 = (f32[1,8,384]{2,1,0:T(8,128)}, f32[1,8,384]{2,1,0:T(8,128)S(1)}, u32[]{:S(2)}) copy-start(f32[1,8,384]{2,1,0:T(8,128)S(1)} %fusion.57) | copy-start | bytes 36868
Sparse Core Ops, SparseCore 0:
  10.3 47.8 all-gather.1
  352.3 91.0 all-reduce.1
where the time goes:
time: 517 us; the launch traced here: 516 us
  waiting for transfers between devices  146 us (28%)
  matrix products  102 us (20%)
  blocking collectives  102 us (20%)
  local copies, waits for them, and re-layouts  75.2 us (15%)
  other arithmetic  51 us (10%)
  starting transfers between devices  23.4 us (5%)
  between operations  16.7 us (3%)
    psum x1, waiting for transfers between devices, local(): feature = lax.psum(partial_feature, 'inp')  90.4 us
    dot_general x1, matrix products, local(): jnp.einsum('mkd,cd->mck', masked, joined_weight, preferred_element_type=j...  82.9 us
    psum x1, blocking collectives, local(): raw_logits = lax.psum(logit_part, 'inp')  58.5 us
    mul x2, local copies, waits for them, and re-layouts, local(): normed.reshape(1, row_count, n_blocks, block_width)  51.8 us
    all_to_all x1, blocking collectives, local(): lax.all_to_all(query_send, 'inp', split_axis=0, concat_axis=2, tiled=True)  43.2 us
    all_to_all x1, waiting for transfers between devices, local(): lax.all_to_all(key_send, 'inp', split_axis=0, concat_axis=2, tiled=True)  31.6 us
    reduce_sum x1, other arithmetic, local(): jnp.mean(activated.reshape(n_masks, n_units, images, PATCHES), axis=-1)  29.6 us
    all_to_all x1, waiting for transfers between devices, local(): lax.all_to_all(value_send, 'inp', split_axis=0, concat_axis=2, tiled=True)  23.1 us
  transfers between devices with their start and end apart: 5, of which 3 were waited for; matrix products, arithmetic and copies ran while one was open for 21% of the time, Pallas kernels for 0%

commit v1 on v0

--- a/solution.py
+++ b/solution.py
@@ -1,14 +1,22 @@
+import functools
 import math
 
 import jax
 import jax.numpy as jnp
 from jax import lax
+from jax.experimental import pallas as pl
+from jax.experimental.pallas import tpu as pltpu
 from jax.sharding import PartitionSpec as P
 
 PATCHES = 256
 
 
 soft_cap = 20.0
+PIPELINED_PARTS = 16
+CHUNKS = 4
+F32 = jnp.float32
+BF16 = jnp.bfloat16
+VMEM_LIMIT = 60 * 1024 * 1024
 
 
 def norm_last(values, gain):
@@ -33,6 +41,416 @@
     mean_probs = jnp.mean(sample_probs, axis=1)
     joint = -jnp.sum(mean_probs * jnp.log(mean_probs), axis=-1)
     return joint - jnp.mean(entropy, axis=1)
+
+
+def permuted(array, bits):
+    count = lax.axis_size("inp")
+    return lax.ppermute(array, "inp", [(i, i ^ bits) for i in range(count)])
+
+
+def gathered_pieces(rows):
+    half = rows.shape[1] // 2
+    first, second = rows[:, :half], rows[:, half:]
+    along_z = jnp.stack([first] + [permuted(first, 4 * k) for k in range(1, 4)])
+    across_y = permuted(along_z, 2)
+    pieces = [
+        (0, [4 * k for k in range(4)], along_z),
+        (0, [4 * k + 2 for k in range(4)], across_y),
+    ]
+    pair = jnp.stack([second, permuted(second, 2)])
+    for k in range(4):
+        moved = pair if k == 0 else permuted(pair, 4 * k)
+        pieces.append((1, [4 * k, 4 * k + 2], moved))
+    return pieces + [
+        (side, [b ^ 1 for b in bits], permuted(array, 1)) for side, bits, array in pieces
+    ]
+
+
+def turn_kernel(layout, me_ref, *refs):
+    sources, out_ref, held = refs[:-2], refs[-2], refs[-1]
+    me = me_ref[0]
+    rows = sources[0].shape[1]
+    half = sources[0].shape[2]
+    for (side, bits), source in zip(layout, sources, strict=True):
+        for at, bit in enumerate(bits):
+            start = pl.multiple_of((me ^ bit) * rows, rows)
+            held[pl.ds(start, rows), side * half : (side + 1) * half] = source[at]
+    for block in range(2 * half // 128):
+        part = held[:, block * 128 : (block + 1) * 128].astype(F32)
+        out_ref[block * 128 : (block + 1) * 128, :] = part.T.astype(BF16)
+
+
+def turned(pieces, me):
+    rows, half = pieces[0][2].shape[1:]
+    total = rows * sum(len(bits) for side, bits, _ in pieces if side == 0)
+    layout = [(side, bits) for side, bits, _ in pieces]
+    return pl.pallas_call(
+        functools.partial(turn_kernel, layout),
+        out_shape=jax.ShapeDtypeStruct((2 * half, total), BF16),
+        in_specs=[pl.BlockSpec(memory_space=pltpu.SMEM)]
+        + [pl.BlockSpec(memory_space=pltpu.VMEM)] * len(pieces),
+        out_specs=pl.BlockSpec(memory_space=pltpu.VMEM),
+        scratch_shapes=[pltpu.VMEM((total, 2 * half), BF16)],
+        compiler_params=pltpu.CompilerParams(vmem_limit_bytes=VMEM_LIMIT),
+        name="turn_rows",
+    )(me.reshape(1), *[array for _, _, array in pieces])
+
+
+def store_masked(norm_ref, gates_ref, masked, first_block, blocks, samples, rows):
+    for block in range(blocks):
+        values = norm_ref[block * 128 : (block + 1) * 128, :].reshape(8, 16, rows)
+        for m in range(samples):
+            gate = gates_ref[m, pl.ds(first_block + block, 1), :]
+            gate = jnp.broadcast_to(gate, (16, rows)).astype(BF16)
+            masked[block * 128 : (block + 1) * 128, m * rows : (m + 1) * rows] = (
+                values * gate[None]
+            ).reshape(128, rows)
+
+
+def query_key_kernel(samples, norm_ref, gates_ref, w_ref, out_ref, masked, total):
+    step = pl.program_id(0)
+    depth, rows = norm_ref.shape
+    blocks = depth // 128
+    comps, kinds, heads, _ = w_ref.shape
+    store_masked(norm_ref, gates_ref, masked, step * blocks, blocks, samples, rows)
+    weight = w_ref[...].reshape(comps * kinds * heads, depth)
+
+    @pl.when(step == 0)
+    def _():
+        total[...] = jnp.zeros_like(total)
+
+    for m in range(samples):
+        product = jnp.dot(
+            weight, masked[:, m * rows : (m + 1) * rows], preferred_element_type=F32
+        )
+        for part in range(rows // 128):
+            total[m * (rows // 128) + part] += product[:, part * 128 : (part + 1) * 128]
+
+    @pl.when(step == pl.num_programs(0) - 1)
+    def _():
+        stride = kinds * heads
+        for h in range(heads):
+            for tile in range(samples * rows // 128):
+                both = [
+                    total.at[tile][pl.ds(t * heads + h, comps, stride=stride), :]
+                    for t in range(kinds)
+                ]
+                m, part = divmod(tile, rows // 128)
+                out_ref[h, m, :, part * 128 : (part + 1) * 128] = jnp.concatenate(
+                    both, axis=0
+                ).astype(BF16)
+
+
+def query_key(norm, gates, w_qkv, first, samples):
+    width, rows = norm.shape
+    comps, _, heads, _ = w_qkv.shape
+    depth = 1024
+    return pl.pallas_call(
+        functools.partial(query_key_kernel, samples),
+        grid=(width // depth,),
+        out_shape=jax.ShapeDtypeStruct((heads, samples, 2 * comps, rows), BF16),
+        in_specs=[
+            pl.BlockSpec((depth, rows), lambda k: (k, 0)),
+            pl.BlockSpec((samples, gates.shape[1], rows), lambda k: (first // samples, 0, 0)),
+            pl.BlockSpec((comps, 2, heads, depth), lambda k: (0, 0, 0, k)),
+        ],
+        out_specs=pl.BlockSpec((heads, samples, 2 * comps, rows), lambda k: (0, 0, 0, 0)),
+        scratch_shapes=[
+            pltpu.VMEM((depth, samples * rows), BF16),
+            pltpu.VMEM((samples * rows // 128, 2 * comps * heads, 128), F32),
+        ],
+        compiler_params=pltpu.CompilerParams(vmem_limit_bytes=VMEM_LIMIT),
+        cost_estimate=pl.CostEstimate(
+            flops=2 * samples * rows * width * 2 * comps * heads,
+            bytes_accessed=2 * (norm.size + 2 * comps * heads * width),
+            transcendentals=0,
+        ),
+        name="query_key",
+    )(norm, gates, w_qkv)
+
+
+def value_kernel(samples, norm_ref, gates_ref, w_ref, out_ref, masked, total):
+    step = pl.program_id(0)
+    depth, rows = norm_ref.shape
+    blocks = depth // 128
+    comps, _, heads, _ = w_ref.shape
+    store_masked(norm_ref, gates_ref, masked, step * blocks, blocks, samples, rows)
+    weight = w_ref[:, 0].reshape(comps * heads, depth)
+
+    @pl.when(step == 0)
+    def _():
+        total[...] = jnp.zeros_like(total)
+
+    for m in range(samples):
+        at = slice(m * rows, (m + 1) * rows)
+        total[:, at] += jnp.dot(weight, masked[:, at], preferred_element_type=F32)
+
+    @pl.when(step == pl.num_programs(0) - 1)
+    def _():
+        for m in range(samples):
+            out_ref[m] = total[:, m * rows : (m + 1) * rows].astype(BF16)
+
+
+def values_of(norm, gates, w_qkv):
+    width, rows = norm.shape
+    samples = gates.shape[0]
+    comps, _, heads, _ = w_qkv.shape
+    depth = 1024
+    return pl.pallas_call(
+        functools.partial(value_kernel, samples),
+        grid=(width // depth,),
+        out_shape=jax.ShapeDtypeStruct((samples, comps * heads, rows), BF16),
+        in_specs=[
+            pl.BlockSpec((depth, rows), lambda k: (k, 0)),
+            pl.BlockSpec(gates.shape, lambda k: (0, 0, 0)),
+            pl.BlockSpec((comps, 1, heads, depth), lambda k: (0, 2, 0, k)),
+        ],
+        out_specs=pl.BlockSpec((samples, comps * heads, rows), lambda k: (0, 0, 0)),
+        scratch_shapes=[
+            pltpu.VMEM((depth, samples * rows), BF16),
+            pltpu.VMEM((comps * heads, samples * rows), F32),
+        ],
+        compiler_params=pltpu.CompilerParams(vmem_limit_bytes=VMEM_LIMIT),
+        cost_estimate=pl.CostEstimate(
+            flops=2 * samples * rows * width * comps * heads,
+            bytes_accessed=2 * (norm.size + comps * heads * width),
+            transcendentals=0,
+        ),
+        name="value_rows",
+    )(norm, gates, w_qkv)
+
+
+def erf(x):
+    x = jnp.clip(x, -4.0, 4.0)
+    s = x * x
+    top = s * -2.72614225801306e-10 + 2.77068142495902e-08
+    for c in (
+        -2.10102402082508e-06,
+        -5.69250639462346e-05,
+        -7.34990630326855e-04,
+        -2.95459980854025e-03,
+        -1.60960333262415e-02,
+    ):
+        top = top * s + c
+    low = s * -1.45660718464996e-05 + -2.13374055278905e-04
+    for c in (-1.68282697438203e-03, -7.37332916720468e-03, -1.42647390514189e-02):
+        low = low * s + c
+    return x * top / low
+
+
+def hidden_kernel(samples, norm_ref, gates_ref, up_ref, down_ref, out_ref, masked, even, odd, sums):
+    step = pl.program_id(0)
+    width, rows = norm_ref.shape
+    lane = lax.broadcasted_iota(jnp.int32, sums.shape, 1)
+
+    @pl.when(step == 0)
+    def _():
+        out_ref[...] = jnp.zeros_like(out_ref)
+
+        @pl.loop(0, width // 128)
+        def _(block):
+            start = pl.multiple_of(block * 128, 128)
+            values = norm_ref[pl.ds(start, 128), :].reshape(8, 16, rows)
+            for m in range(samples):
+                gate = jnp.broadcast_to(gates_ref[m, pl.ds(block, 1), :], (16, rows))
+                masked[m, pl.ds(start, 128), :] = (values * gate.astype(BF16)[None]).reshape(
+                    128, rows
+                )
+
+    def pool(held, m):
+        v = held[...]
+        active = (0.5 * v) * (1.0 + erf(v * math.sqrt(0.5)))
+        pooled = jnp.sum(active, axis=1, keepdims=True) * (1.0 / rows)
+        sums[...] = jnp.where(lane == m, pooled, sums[...])
+
+    odd[...] = jnp.zeros_like(odd)
+    sums[...] = jnp.zeros_like(sums)
+
+    @pl.loop(0, samples // 2)
+    def _(pair):
+        even[...] = jnp.dot(up_ref[...], masked[2 * pair], preferred_element_type=F32)
+        pool(odd, 2 * pair - 1)
+        odd[...] = jnp.dot(up_ref[...], masked[2 * pair + 1], preferred_element_type=F32)
+        pool(even, 2 * pair)
+
+    pool(odd, samples - 1)
+    pooled = sums[...].T[:16].astype(BF16)
+    out_ref[...] += jnp.dot(pooled, down_ref[...], preferred_element_type=F32)[:samples]
+
+
+def hidden_part(norm, gates, w_up, w_down):
+    width, rows = norm.shape
+    samples = gates.shape[0]
+    units = w_up.shape[0]
+    tile = 256
+    return pl.pallas_call(
+        functools.partial(hidden_kernel, samples),
+        grid=(units // tile,),
+        out_shape=jax.ShapeDtypeStruct((samples, width), F32),
+        in_specs=[
+            pl.BlockSpec(norm.shape, lambda i: (0, 0)),
+            pl.BlockSpec(gates.shape, lambda i: (0, 0, 0)),
+            pl.BlockSpec((tile, width), lambda i: (i, 0)),
+            pl.BlockSpec((tile, width), lambda i: (i, 0)),
+        ],
+        out_specs=pl.BlockSpec((samples, width), lambda i: (0, 0)),
+        scratch_shapes=[
+            pltpu.VMEM((samples, width, rows), BF16),
+            pltpu.VMEM((tile, rows), F32),
+            pltpu.VMEM((tile, rows), F32),
+            pltpu.VMEM((tile, 128), F32),
+        ],
+        compiler_params=pltpu.CompilerParams(vmem_limit_bytes=VMEM_LIMIT),
+        cost_estimate=pl.CostEstimate(
+            flops=2 * samples * rows * width * units,
+            bytes_accessed=2 * (norm.size + 2 * units * width),
+            transcendentals=samples * rows * units,
+        ),
+        name="hidden_part",
+    )(norm, gates, w_up, w_down)
+
+
+def attention_kernel(items, x_ref, query_gain_ref, key_gain_ref, out_ref):
+    parts, _, both, rows = x_ref.shape
+    comps = both // 2
+    head_dim = parts * comps
+
+    def normed(values, gain_ref):
+        values = values.reshape(head_dim, rows)
+        average = jnp.mean(values, axis=0, keepdims=True)
+        centered = values - average
+        spread_sq = jnp.mean(centered * centered, axis=0, keepdims=True)
+        return (centered * lax.rsqrt(spread_sq + 1e-06) * gain_ref[...]).astype(BF16)
+
+    for j in range(items):
+        x = x_ref[:, j].astype(F32)
+        query = normed(x[:, :comps], query_gain_ref)
+        key = normed(x[:, comps:], key_gain_ref)
+        scores = lax.dot_general(
+            query, key, (((0,), (0,)), ((), ())), preferred_element_type=F32
+        ) * (1.0 / math.sqrt(head_dim))
+        e = jnp.exp(scores)
+        weights = (e / jnp.sum(e, axis=1, keepdims=True)).astype(BF16)
+        out_ref[j : j + 1, :] = jnp.sum(weights.astype(F32), axis=0, keepdims=True) * (1.0 / rows)
+
+
+def key_weights(exchanged, query_gain, key_gain):
+    parts, items, both, rows = exchanged.shape
+    head_dim = parts * both // 2
+    return pl.pallas_call(
+        functools.partial(attention_kernel, items),
+        out_shape=jax.ShapeDtypeStruct((items, rows), F32),
+        compiler_params=pltpu.CompilerParams(vmem_limit_bytes=VMEM_LIMIT),
+        cost_estimate=pl.CostEstimate(
+            flops=2 * items * rows * rows * head_dim,
+            bytes_accessed=2 * exchanged.size,
+            transcendentals=items * rows * rows,
+        ),
+        name="key_weights",
+    )(exchanged, query_gain.reshape(head_dim, 1), key_gain.reshape(head_dim, 1))
+
+
+def pooled_logits(feature, final_gain, w_head):
+    highest = lax.Precision.HIGHEST
+    gain_head = jnp.dot(final_gain[None], w_head.astype(F32), precision=highest)
+    mean = jnp.mean(feature, axis=-1, keepdims=True)
+    centered = feature - mean
+    spread = jnp.sum(centered * centered, axis=-1, keepdims=True)
+    logits = jnp.dot(centered * final_gain, w_head.astype(F32), precision=highest)
+    columns = feature.shape[1]
+    samples, classes = logits.shape
+    bits = 1
+    while bits < lax.axis_size("inp"):
+        sent = jnp.concatenate(
+            [
+                jnp.concatenate([logits, mean, spread], axis=1),
+                jnp.pad(gain_head, ((0, 0), (0, 2))),
+            ],
+            axis=0,
+        )
+        other = permuted(sent, bits)
+        other_mean = other[:samples, classes : classes + 1]
+        joint = 0.5 * (mean + other_mean)
+        logits = (
+            logits
+            + other[:samples, :classes]
+            + (mean - joint) * gain_head
+            + (other_mean - joint) * other[samples:, :classes]
+        )
+        gap = mean - other_mean
+        spread = spread + other[:samples, classes + 1 :] + gap * gap * (0.5 * columns)
+        gain_head = gain_head + other[samples:, :classes]
+        mean = joint
+        columns = 2 * columns
+        bits = 2 * bits
+    scale = lax.rsqrt(spread / columns + 1e-06)
+    return mean, scale, logits * scale
+
+
+def pipelined(
+    tokens,
+    dropout_masks,
+    input_gain,
+    w_qkv,
+    w_up,
+    query_gain,
+    key_gain,
+    w_proj,
+    w_down,
+    final_gain,
+    w_head,
+):
+    n_parts = lax.axis_size("inp")
+    me = lax.axis_index("inp")
+    model_width = tokens.shape[1]
+    n_masks, all_rows, _ = dropout_masks.shape
+    n_comps, _, n_heads, _ = w_qkv.shape
+    own = norm_last(tokens.astype(F32), input_gain).astype(BF16)
+    gates = 2.0 * jnp.transpose(dropout_masks, (0, 2, 1)).astype(F32)
+    norm = turned(gathered_pieces(own), me)
+    samples = n_masks // CHUNKS
+    heads_dev = n_heads // n_parts
+    items = heads_dev * samples
+    exchanged = []
+    for chunk in range(CHUNKS):
+        both = query_key(norm, gates, w_qkv, chunk * samples, samples)
+        both = both.reshape(n_parts, items, 2 * n_comps, all_rows)
+        exchanged.append(lax.all_to_all(both, "inp", split_axis=0, concat_axis=0, tiled=True))
+    value = values_of(norm, gates, w_qkv)
+    hidden = hidden_part(norm, gates, w_up, w_down)
+    key_mean = jnp.concatenate([key_weights(x, query_gain, key_gain) for x in exchanged], axis=0)
+    key_mean = lax.all_to_all(
+        jnp.broadcast_to(key_mean[None], (n_parts,) + key_mean.shape),
+        "inp",
+        split_axis=0,
+        concat_axis=0,
+        tiled=True,
+    )
+    key_mean = key_mean.reshape(n_parts, CHUNKS, heads_dev, samples, all_rows)
+    key_mean = jnp.transpose(key_mean, (1, 3, 0, 2, 4)).reshape(n_masks, 1, n_heads, all_rows)
+    value = value.reshape(n_masks, n_comps, n_heads, all_rows).astype(F32)
+    attended = jnp.sum(value * key_mean, axis=-1).astype(BF16).reshape(n_masks, n_comps * n_heads)
+    mixed_sum = jnp.dot(
+        attended, w_proj.reshape(n_comps * n_heads, model_width), preferred_element_type=F32
+    )
+    input_sum = jnp.sum(tokens.astype(F32), axis=0, keepdims=True) / all_rows
+    partial_feature = mixed_sum + hidden + input_sum
+    slice_width = model_width // n_parts
+    feature = jnp.sum(
+        lax.all_to_all(
+            partial_feature.reshape(n_masks, n_parts, slice_width),
+            "inp",
+            split_axis=1,
+            concat_axis=0,
+            tiled=True,
+        ).reshape(n_parts, n_masks, slice_width),
+        axis=0,
+    )
+    gain = lax.dynamic_slice_in_dim(final_gain, me * slice_width, slice_width, 0)
+    mean, scale, raw_logits = pooled_logits(feature, gain, w_head)
+    embedding = (feature - mean) * scale * gain
+    logits = soft_cap * jnp.tanh(raw_logits / soft_cap)
+    return (embedding[None], bald_score(logits[None]))
 
 
 def local(
@@ -137,8 +555,9 @@
 
 
 def solution(mesh):
+    fits = mesh.shape["inp"] == PIPELINED_PARTS
     return jax.shard_map(
-        local,
+        pipelined if fits else local,
         mesh=mesh,
         in_specs=(
             P(("groups", "inp"), None),

time: 517 us -> 282 us (0.55)
  Pallas kernels: 0 us -> 144 us
  blocking collectives: 102 us -> 0 us
  matrix products: 102 us -> 5.32 us
  waiting for transfers between devices: 146 us -> 61.1 us
  local copies, waits for them, and re-layouts: 75.2 us -> 5.83 us
  other arithmetic: 51 us -> 12 us
  starting transfers between devices: 23.4 us -> 48.8 us
  between operations: 16.7 us -> 3.48 us
    pallas_call x0 -> x11, Pallas kernels: none -> 144 us  [the longest x1 64.5 us: hidden_part(): pl.pallas_call(functools.partial(hidden_kernel, samples), grid=(units //...]
    dot_general x7 -> x3, matrix products: 102 us -> 5.32 us  [the longest x1 3.83 us: pipelined(): jnp.dot(attended, w_proj.reshape(n_comps * n_heads, model_width), preferr...]
    psum x1 -> x0, waiting for transfers between devices: 90.4 us -> none  [local(): feature = lax.psum(partial_feature, 'inp')]
    psum x1 -> x0, blocking collectives: 58.5 us -> none  [local(): raw_logits = lax.psum(logit_part, 'inp')]
    mul x2, local copies, waits for them, and re-layouts: 51.8 us -> 0.47 us  [pipelined(): value * key_mean]
    all_to_all x1 -> x0, blocking collectives: 43.2 us -> none  [local(): lax.all_to_all(query_send, 'inp', split_axis=0, concat_axis=2, tiled=True)]
    reduce_sum x7 -> x4, other arithmetic: 37.8 us -> 3.44 us  [the longest x1 1.9 us: pipelined(): jnp.sum(value * key_mean, axis=-1).astype(BF16)]
    ppermute x0 -> x18, waiting for transfers between devices: none -> 33.5 us  [permuted(): return lax.ppermute(array, 'inp', [(i, i ^ bits) for i in range(count)])]
  transfers between devices with their start and end apart: 5 -> 24, of which waited for: 3 -> 11; matrix products, arithmetic and copies ran while one was open for 21% -> 2% of each run, Pallas kernels for 0% -> 44%
where the time goes in v1:
time: 282 us; the launch traced here: 281 us
  Pallas kernels  144 us (51%)
  waiting for transfers between devices  61.1 us (22%)
  starting transfers between devices  48.8 us (17%)
  other arithmetic  12 us (4%)
  local copies, waits for them, and re-layouts  5.83 us (2%)
  matrix products  5.32 us (2%)
  between operations  3.48 us (1%)
    pallas_call x1, Pallas kernels, hidden_part(): pl.pallas_call(functools.partial(hidden_kernel, samples), grid=(units //...  64.5 us
    pallas_call x4, Pallas kernels, query_key(): pl.pallas_call(functools.partial(query_key_kernel, samples), grid=(width...  45.9 us
    ppermute x18, waiting for transfers between devices, permuted(): return lax.ppermute(array, 'inp', [(i, i ^ bits) for i in range(count)])  33.5 us
    all_to_all x4, starting transfers between devices, pipelined(): lax.all_to_all(both, 'inp', split_axis=0, concat_axis=0, tiled=True)  21.4 us
    all_to_all x4, waiting for transfers between devices, pipelined(): lax.all_to_all(both, 'inp', split_axis=0, concat_axis=0, tiled=True)  20.2 us
    pallas_call x1, Pallas kernels, values_of(): pl.pallas_call(functools.partial(value_kernel, samples), grid=(width // d...  16.6 us
    ppermute x18, starting transfers between devices, permuted(): return lax.ppermute(array, 'inp', [(i, i ^ bits) for i in range(count)])  15.4 us
    pallas_call x4, Pallas kernels, key_weights(): pl.pallas_call(functools.partial(attention_kernel, items), out_shape=jax....  12.5 us
  transfers between devices with their start and end apart: 24, of which 11 were waited for; matrix products, arithmetic and copies ran while one was open for 2% of the time, Pallas kernels for 44%

profile of v1, /device:TPU:0, one launch (start us, length us, event | category | flops | bytes accessed | tf_op | source)
XLA Modules:
  0.0 280.7 jit_solution(9020074614560758087)
XLA Ops:
  0.6 1.2 convert_reduce_fusion.1
  1.8 1.2 convert_reduce_fusion
  3.0 1.1 fusion.5
  4.1 3.1 %collective-permute-start = (bf16[16,3072]{1,0:T(8,128)(2,1)S(1)}, bf16[16,3072]{1,0:T(8,128)(2,1)S(1)}, u32[]{:S(2)}, u32[]{:S(2)}) collective-permute-start(bf16[16,3072]{1,0:T(8,128)(2,1)S(1)} %get-tuple-element.26), channel_id=1, source_target_pairs={{0,4},{1,5},{2,6},{3,7},{4,0},{5,1},{6,2},{7,3},{8,12},{9,13},{10,... | collective-permute-start | bytes 294920 | tf_op jit(solution)/shard_map/ppermute | solution.py:48
  7.2 2.6 collective-permute-start.1
  9.8 1.7 collective-permute-start.4
  11.5 6.1 %collective-permute-done.1 = bf16[16,3072]{1,0:T(8,128)(2,1)S(1)} collective-permute-done((bf16[16,3072]{1,0:T(8,128)(2,1)S(1)}, bf16[16,3072]{1,0:T(8,128)(2,1)S(1)}, u32[]{:S(2)}, u32[]{:S(2)}) %collective-permute-start.1) | collective-permute-done | bytes 98336 | tf_op jit(solution)/shard_map/ppermute | solution.py:48
  17.7 1.6 collective-permute-start.3
  19.3 1.7 collective-permute-start.5
  21.0 1.4 collective-permute-start.6
  22.4 1.3 collective-permute-start.7
  23.8 3.4 %collective-permute-done.5.refs_3_ = bf16[2,16,3072]{2,1,0:T(8,128)(2,1)S(1)} collective-permute-done((bf16[2,16,3072]{2,1,0:T(8,128)(2,1)S(1)}, bf16[2,16,3072]{2,1,0:T(8,128)(2,1)S(1)}, u32[]{:S(2)}, u32[]{:S(2)}) %collective-permute-start.5) | collective-permute-done | bytes 196640 | tf_op jit(solution)/shard_map/ppermute | solution.py:48
  27.2 0.5 collective-permute-start.9
  27.7 9.6 %collective-permute-done.6.refs_4_ = bf16[2,16,3072]{2,1,0:T(8,128)(2,1)S(1)} collective-permute-done((bf16[2,16,3072]{2,1,0:T(8,128)(2,1)S(1)}, bf16[2,16,3072]{2,1,0:T(8,128)(2,1)S(1)}, u32[]{:S(2)}, u32[]{:S(2)}) %collective-permute-start.6) | collective-permute-done | bytes 196640 | tf_op jit(solution)/shard_map/ppermute | solution.py:48
  37.4 0.5 collective-permute-start.12
  38.0 1.8 multiply_bitcast_fusion.gates_ref
  39.9 0.6 copy-done.8
  40.9 4.6 %turn_rows.1.norm_ref = bf16[6144,256]{1,0:T(8,128)(2,1)} custom-call(s32[1]{0:T(128)} %bitcast.me_ref, bf16[4,16,3072]{2,1,0:T(8,128)(2,1)} %copy-done.5, bf16[4,16,3072]{2,1,0:T(8,128)(2,1)} %copy-done.7, bf16[2,16,3072]{2,1,0:T(8,128)(2,1)} %copy-done.6, bf16[2,16,3072]{2,1,0:T(8,128)(2,1)} %copy-done.10, bf16[2,16,3072]{2,1,0:T(8,128)(2,1)} %copy-done.11, ...), custom_call_target="tpu_custom_call" | custom-call | tf_op jit(solution)/shard_map/turn_rows/pallas_call | solution.py:87
  45.4 11.5 %query_key.4 = bf16[48,2,16,256]{3,2,1,0:T(8,128)(2,1)} custom-call(bf16[6144,256]{1,0:T(8,128)(2,1)} %turn_rows.1.norm_ref, f32[8,48,256]{2,1,0:T(8,128)} %multiply_bitcast_fusion.gates_ref, bf16[8,3,48,6144]{3,2,1,0:T(8,128)(2,1)} %w_ref.9), custom_call_target="tpu_custom_call" | custom-call | flops 4831838208 | bytes 12582912 | tf_op jit(solution)/shard_map/query_key/pallas_call | solution.py:148
  56.9 4.9 %all-to-all-start = ((bf16[16,6,16,256]{3,2,1,0:T(8,128)(2,1)}), bf16[16,6,16,256]{3,2,1,0:T(8,128)(2,1)S(1)}, u32[]{:S(2)}, u32[]{:S(2)}) async-start(bf16[16,6,16,256]{3,2,1,0:T(8,128)(2,1)} %bitcast.52), calls=%async_computation | async-start | bytes 1572864 | tf_op jit(solution)/shard_map/all_to_all | solution.py:418
  61.9 11.5 %query_key.5 = bf16[48,2,16,256]{3,2,1,0:T(8,128)(2,1)} custom-call(bf16[6144,256]{1,0:T(8,128)(2,1)} %turn_rows.1.norm_ref, f32[8,48,256]{2,1,0:T(8,128)} %multiply_bitcast_fusion.gates_ref, bf16[8,3,48,6144]{3,2,1,0:T(8,128)(2,1)} %w_ref.9), custom_call_target="tpu_custom_call" | custom-call | flops 4831838208 | bytes 12582912 | tf_op jit(solution)/shard_map/query_key/pallas_call | solution.py:148
  73.4 7.2 %all-to-all-done.x_ref = bf16[16,6,16,256]{3,2,1,0:T(8,128)(2,1)S(1)} async-done(((bf16[16,6,16,256]{3,2,1,0:T(8,128)(2,1)}), bf16[16,6,16,256]{3,2,1,0:T(8,128)(2,1)S(1)}, u32[]{:S(2)}, u32[]{:S(2)}) %all-to-all-start) | async-done | bytes 786464 | tf_op jit(solution)/shard_map/all_to_all | solution.py:418
  80.6 5.5 %all-to-all-start.1 = ((bf16[16,6,16,256]{3,2,1,0:T(8,128)(2,1)}), bf16[16,6,16,256]{3,2,1,0:T(8,128)(2,1)S(1)}, u32[]{:S(2)}, u32[]{:S(2)}) async-start(bf16[16,6,16,256]{3,2,1,0:T(8,128)(2,1)} %bitcast.51), calls=%async_computation.1 | async-start | bytes 1572864 | tf_op jit(solution)/shard_map/all_to_all | solution.py:418
  86.1 11.5 %query_key.6 = bf16[48,2,16,256]{3,2,1,0:T(8,128)(2,1)} custom-call(bf16[6144,256]{1,0:T(8,128)(2,1)} %turn_rows.1.norm_ref, f32[8,48,256]{2,1,0:T(8,128)} %multiply_bitcast_fusion.gates_ref, bf16[8,3,48,6144]{3,2,1,0:T(8,128)(2,1)} %w_ref.9), custom_call_target="tpu_custom_call" | custom-call | flops 4831838208 | bytes 12582912 | tf_op jit(solution)/shard_map/query_key/pallas_call | solution.py:148
  97.6 7.2 %all-to-all-done.1.x_ref = bf16[16,6,16,256]{3,2,1,0:T(8,128)(2,1)S(1)} async-done(((bf16[16,6,16,256]{3,2,1,0:T(8,128)(2,1)}), bf16[16,6,16,256]{3,2,1,0:T(8,128)(2,1)S(1)}, u32[]{:S(2)}, u32[]{:S(2)}) %all-to-all-start.1) | async-done | bytes 786464 | tf_op jit(solution)/shard_map/all_to_all | solution.py:418
  104.8 5.5 %all-to-all-start.2 = ((bf16[16,6,16,256]{3,2,1,0:T(8,128)(2,1)}), bf16[16,6,16,256]{3,2,1,0:T(8,128)(2,1)S(1)}, u32[]{:S(2)}, u32[]{:S(2)}) async-start(bf16[16,6,16,256]{3,2,1,0:T(8,128)(2,1)} %bitcast.50), calls=%async_computation.2 | async-start | bytes 1572864 | tf_op jit(solution)/shard_map/all_to_all | solution.py:418
  110.3 0.7 copy.44.query_gain_ref
  111.0 0.7 copy.45.key_gain_ref
  111.7 11.5 %query_key.7 = bf16[48,2,16,256]{3,2,1,0:T(8,128)(2,1)} custom-call(bf16[6144,256]{1,0:T(8,128)(2,1)} %turn_rows.1.norm_ref, f32[8,48,256]{2,1,0:T(8,128)} %multiply_bitcast_fusion.gates_ref, bf16[8,3,48,6144]{3,2,1,0:T(8,128)(2,1)} %w_ref.9), custom_call_target="tpu_custom_call" | custom-call | flops 4831838208 | bytes 12582912 | tf_op jit(solution)/shard_map/query_key/pallas_call | solution.py:148
  123.2 5.7 %all-to-all-done.2.x_ref = bf16[16,6,16,256]{3,2,1,0:T(8,128)(2,1)S(1)} async-done(((bf16[16,6,16,256]{3,2,1,0:T(8,128)(2,1)}), bf16[16,6,16,256]{3,2,1,0:T(8,128)(2,1)S(1)}, u32[]{:S(2)}, u32[]{:S(2)}) %all-to-all-start.2) | async-done | bytes 786464 | tf_op jit(solution)/shard_map/all_to_all | solution.py:418
  129.0 5.5 %all-to-all-start.3 = ((bf16[16,6,16,256]{3,2,1,0:T(8,128)(2,1)}), bf16[16,6,16,256]{3,2,1,0:T(8,128)(2,1)S(1)}, u32[]{:S(2)}, u32[]{:S(2)}) async-start(bf16[16,6,16,256]{3,2,1,0:T(8,128)(2,1)} %bitcast.49), calls=%async_computation.3 | async-start | bytes 1572864 | tf_op jit(solution)/shard_map/all_to_all | solution.py:418
  134.5 64.5 %hidden_part.1 = f32[8,6144]{1,0:T(8,128)} custom-call(bf16[6144,256]{1,0:T(8,128)(2,1)} %turn_rows.1.norm_ref, f32[8,48,256]{2,1,0:T(8,128)} %multiply_bitcast_fusion.gates_ref, bf16[1536,6144]{1,0:T(8,128)(2,1)} %up_ref.1, bf16[1536,6144]{1,0:T(8,128)(2,1)} %down_ref.1), custom_call_target="tpu_custom_call" | custom-call | flops 38654705664 | bytes 40894464 | tf_op jit(solution)/shard_map/hidden_part/pallas_call | solution.py:286
  199.0 3.1 %key_weights.4 = f32[6,256]{1,0:T(8,128)} custom-call(bf16[16,6,16,256]{3,2,1,0:T(8,128)(2,1)} %copy-done.1, f32[128,1]{1,0:T(8,128)} %copy.44.query_gain_ref, f32[128,1]{1,0:T(8,128)} %copy.45.key_gain_ref), custom_call_target="tpu_custom_call" | custom-call | flops 100663296 | bytes 786432 | tf_op jit(solution)/shard_map/key_weights/pallas_call | solution.py:340
  202.1 3.1 %key_weights.5 = f32[6,256]{1,0:T(8,128)} custom-call(bf16[16,6,16,256]{3,2,1,0:T(8,128)(2,1)} %copy-done.2, f32[128,1]{1,0:T(8,128)} %copy.44.query_gain_ref, f32[128,1]{1,0:T(8,128)} %copy.45.key_gain_ref), custom_call_target="tpu_custom_call" | custom-call | flops 100663296 | bytes 786432 | tf_op jit(solution)/shard_map/key_weights/pallas_call | solution.py:340
  205.2 3.1 %key_weights.6 = f32[6,256]{1,0:T(8,128)} custom-call(bf16[16,6,16,256]{3,2,1,0:T(8,128)(2,1)} %copy-done.3, f32[128,1]{1,0:T(8,128)} %copy.44.query_gain_ref, f32[128,1]{1,0:T(8,128)} %copy.45.key_gain_ref), custom_call_target="tpu_custom_call" | custom-call | flops 100663296 | bytes 786432 | tf_op jit(solution)/shard_map/key_weights/pallas_call | solution.py:340
  208.3 0.9 copy-done.4
  209.2 3.1 %key_weights.7 = f32[6,256]{1,0:T(8,128)} custom-call(bf16[16,6,16,256]{3,2,1,0:T(8,128)(2,1)} %copy-done.4, f32[128,1]{1,0:T(8,128)} %copy.44.query_gain_ref, f32[128,1]{1,0:T(8,128)} %copy.45.key_gain_ref), custom_call_target="tpu_custom_call" | custom-call | flops 100663296 | bytes 786432 | tf_op jit(solution)/shard_map/key_weights/pallas_call | solution.py:340
  212.3 0.8 pad_maximum_fusion.2
  213.1 0.8 broadcast_in_dim.4
  213.8 6.0 %all-to-all-start.4 = ((f32[16,24,256]{2,1,0:T(8,128)}), f32[16,24,256]{2,1,0:T(8,128)S(1)}, u32[]{:S(2)}, u32[]{:S(2)}) async-start(f32[16,24,256]{2,1,0:T(8,128)} %broadcast_in_dim.4), calls=%async_computation.4 | async-start | bytes 786432 | tf_op jit(solution)/shard_map/all_to_all | solution.py:422
  219.9 16.6 %value_rows.1 = bf16[8,384,256]{2,1,0:T(8,128)(2,1)} custom-call(bf16[6144,256]{1,0:T(8,128)(2,1)} %turn_rows.1.norm_ref, f32[8,48,256]{2,1,0:T(8,128)} %multiply_bitcast_fusion.gates_ref, bf16[8,3,48,6144]{3,2,1,0:T(8,128)(2,1)} %w_ref.9), custom_call_target="tpu_custom_call" | custom-call | flops 9663676416 | bytes 7864320 | tf_op jit(solution)/shard_map/value_rows/pallas_call | solution.py:199
  236.6 0.3 copy.62
  236.9 0.2 reshape.213
  237.1 1.9 fusion
  239.1 3.8 %add_add_fusion = f32[8,6144]{1,0:T(8,128)} fusion(f32[8,6144]{1,0:T(8,128)S(1)} %copy-done.14, f32[6144]{0:T(1024)S(1)} %broadcast_multiply_fusion, bf16[8,48,6144]{2,1,0:T(8,128)(2,1)} %param.18, bf16[8,8,48]{2,1,0:T(8,128)(2,1)S(1)} %convert_element_type.33), kind=kOutput, calls=%fused_computation.14 | convolution fusion | flops 37847040 | bytes 5142528 | tf_op jit(solution)/shard_map/dot_general | solution.py:433
  242.9 6.0 %all-to-all-start.5 = ((f32[8,16,384]{2,0,1:T(8,128)}), f32[8,16,384]{2,0,1:T(8,128)S(1)}, u32[]{:S(2)}, u32[]{:S(2)}) async-start(f32[8,16,384]{2,0,1:T(8,128)} %bitcast.18), calls=%async_computation.5 | async-start | bytes 393216 | tf_op jit(solution)/shard_map/all_to_all | solution.py:440
  248.9 0.8 dynamic_slice.3
  249.7 0.7 fusion.43
  250.5 7.5 %all-to-all-done.5 = f32[8,16,384]{2,0,1:T(8,128)S(1)} async-done(((f32[8,16,384]{2,0,1:T(8,128)}), f32[8,16,384]{2,0,1:T(8,128)S(1)}, u32[]{:S(2)}, u32[]{:S(2)}) %all-to-all-start.5) | async-done | bytes 196640 | tf_op jit(solution)/shard_map/all_to_all | solution.py:440
  258.1 0.8 fusion.22
  258.8 0.2 multiply_reduce_fusion.1
  259.3 1.2 collective-permute-done.14
  260.6 0.2 subtract_reduce_fusion.7
  260.9 4.3 %collective-permute-done.15 = f32[9,1002]{1,0:T(8,128)S(1)} collective-permute-done((f32[9,1002]{1,0:T(8,128)S(1)}, f32[9,1002]{1,0:T(8,128)S(1)}, u32[]{:S(2)}, u32[]{:S(2)}) %collective-permute-start.15) | collective-permute-done | bytes 36104 | tf_op jit(solution)/shard_map/ppermute | solution.py:48
  265.2 0.2 subtract_reduce_fusion.5
  265.7 4.1 %collective-permute-done.16 = f32[9,1002]{1,0:T(8,128)S(1)} collective-permute-done((f32[9,1002]{1,0:T(8,128)S(1)}, f32[9,1002]{1,0:T(8,128)S(1)}, u32[]{:S(2)}, u32[]{:S(2)}) %collective-permute-start.16) | collective-permute-done | bytes 36104 | tf_op jit(solution)/shard_map/ppermute | solution.py:48
  270.1 0.7 collective-permute-start.17
  270.9 4.7 %collective-permute-done.17 = f32[9,1002]{1,0:T(8,128)S(1)} collective-permute-done((f32[9,1002]{1,0:T(8,128)S(1)}, f32[9,1002]{1,0:T(8,128)S(1)}, u32[]{:S(2)}, u32[]{:S(2)}) %collective-permute-start.17) | collective-permute-done | bytes 36104 | tf_op jit(solution)/shard_map/ppermute | solution.py:48
  275.6 0.2 subtract_reduce_fusion.1
  275.8 0.2 exponential_reduce_fusion
  276.0 0.2 multiply_reduce_fusion
  276.2 0.7 subtract_reduce_fusion.8
  276.9 0.6 fusion.27
  278.2 0.7 fusion.21
  (84 shorter events, 2.2 us)
Async XLA Ops:
  0.6 249.1 %copy-start = (bf16[384,1000]{0,1:T(8,128)(2,1)S(1)}, bf16[384,1000]{0,1:T(8,128)(2,1)}, u32[]{:S(2)}) copy-start(bf16[384,1000]{0,1:T(8,128)(2,1)} %param.21) | copy-start | bytes 2304004
  4.1 7.4 %collective-permute-start = (bf16[16,3072]{1,0:T(8,128)(2,1)S(1)}, bf16[16,3072]{1,0:T(8,128)(2,1)S(1)}, u32[]{:S(2)}, u32[]{:S(2)}) collective-permute-start(bf16[16,3072]{1,0:T(8,128)(2,1)S(1)} %get-tuple-element.26), channel_id=1, source_target_pairs={{0,4},{1,5},{2,6},{3,7},{4,0},{5,1},{6,2},{7,3},{8,12},{9,13},{10,... | collective-permute-start | bytes 294920 | tf_op jit(solution)/shard_map/ppermute | solution.py:48
  7.2 10.4 %collective-permute-start.1 = (bf16[16,3072]{1,0:T(8,128)(2,1)S(1)}, bf16[16,3072]{1,0:T(8,128)(2,1)S(1)}, u32[]{:S(2)}, u32[]{:S(2)}) collective-permute-start(bf16[16,3072]{1,0:T(8,128)(2,1)S(1)} %get-tuple-element.26), channel_id=1, source_target_pairs={{0,8},{1,9},{2,10},{3,11},{4,12},{5,13},{6,14},{7,15},{8,0},{9,1},... | collective-permute-start | bytes 294920 | tf_op jit(solution)/shard_map/ppermute | solution.py:48
  9.8 7.8 %collective-permute-start.2 = (bf16[16,3072]{1,0:T(8,128)(2,1)S(1)}, bf16[16,3072]{1,0:T(8,128)(2,1)S(1)}, u32[]{:S(2)}, u32[]{:S(2)}) collective-permute-start(bf16[16,3072]{1,0:T(8,128)(2,1)S(1)} %get-tuple-element.26), channel_id=1, source_target_pairs={{0,12},{1,13},{2,14},{3,15},{4,8},{5,9},{6,10},{7,11},{8,4},{9,5},... | collective-permute-start | bytes 294920 | tf_op jit(solution)/shard_map/ppermute | solution.py:48
  9.8 9.5 %collective-permute-start.4 = (bf16[16,3072]{1,0:T(8,128)(2,1)S(1)}, bf16[16,3072]{1,0:T(8,128)(2,1)S(1)}, u32[]{:S(2)}, u32[]{:S(2)}) collective-permute-start(bf16[16,3072]{1,0:T(8,128)(2,1)S(1)} %get-tuple-element.25), channel_id=1, source_target_pairs={{0,2},{1,3},{2,0},{3,1},{4,6},{5,7},{6,4},{7,5},{8,10},{9,11},{10,... | collective-permute-start | bytes 294920 | tf_op jit(solution)/shard_map/ppermute | solution.py:48
  17.7 22.1 %copy-start.5 = (bf16[4,16,3072]{2,1,0:T(8,128)(2,1)}, bf16[4,16,3072]{2,1,0:T(8,128)(2,1)S(1)}, u32[]{:S(2)}) copy-start(bf16[4,16,3072]{2,1,0:T(8,128)(2,1)S(1)} %pad_maximum_fusion.refs_0_) | copy-start | bytes 1179652
  17.7 9.5 %collective-permute-start.3 = (bf16[4,16,3072]{2,1,0:T(8,128)(2,1)S(1)}, bf16[4,16,3072]{2,1,0:T(8,128)(2,1)S(1)}, u32[]{:S(2)}, u32[]{:S(2)}) collective-permute-start(bf16[4,16,3072]{2,1,0:T(8,128)(2,1)S(1)} %pad_maximum_fusion.refs_0_), channel_id=1, source_target_pairs={{0,2},{1,3},{2,0},{3,1},{4,6},{5,7},{6,4},{7,5},{8,10},{9,11},{10,... | collective-permute-start | bytes 1179656 | tf_op jit(solution)/shard_map/ppermute | solution.py:48
  19.3 20.5 %copy-start.6 = (bf16[2,16,3072]{2,1,0:T(8,128)(2,1)}, bf16[2,16,3072]{2,1,0:T(8,128)(2,1)S(1)}, u32[]{:S(2)}) copy-start(bf16[2,16,3072]{2,1,0:T(8,128)(2,1)S(1)} %pad_maximum_fusion.1.refs_2_) | copy-start | bytes 589828
  19.3 7.9 %collective-permute-start.5 = (bf16[2,16,3072]{2,1,0:T(8,128)(2,1)S(1)}, bf16[2,16,3072]{2,1,0:T(8,128)(2,1)S(1)}, u32[]{:S(2)}, u32[]{:S(2)}) collective-permute-start(bf16[2,16,3072]{2,1,0:T(8,128)(2,1)S(1)} %pad_maximum_fusion.1.refs_2_), channel_id=1, source_target_pairs={{0,4},{1,5},{2,6},{3,7},{4,0},{5,1},{6,2},{7,3},{8,12},{9,13},{10,... | collective-permute-start | bytes 589832 | tf_op jit(solution)/shard_map/ppermute | solution.py:48
  21.0 16.4 %collective-permute-start.6 = (bf16[2,16,3072]{2,1,0:T(8,128)(2,1)S(1)}, bf16[2,16,3072]{2,1,0:T(8,128)(2,1)S(1)}, u32[]{:S(2)}, u32[]{:S(2)}) collective-permute-start(bf16[2,16,3072]{2,1,0:T(8,128)(2,1)S(1)} %pad_maximum_fusion.1.refs_2_), channel_id=1, source_target_pairs={{0,8},{1,9},{2,10},{3,11},{4,12},{5,13},{6,14},{7,15},{8,0},{9,1},... | collective-permute-start | bytes 589832 | tf_op jit(solution)/shard_map/ppermute | solution.py:48
  22.4 14.9 %collective-permute-start.7 = (bf16[2,16,3072]{2,1,0:T(8,128)(2,1)S(1)}, bf16[2,16,3072]{2,1,0:T(8,128)(2,1)S(1)}, u32[]{:S(2)}, u32[]{:S(2)}) collective-permute-start(bf16[2,16,3072]{2,1,0:T(8,128)(2,1)S(1)} %pad_maximum_fusion.1.refs_2_), channel_id=1, source_target_pairs={{0,12},{1,13},{2,14},{3,15},{4,8},{5,9},{6,10},{7,11},{8,4},{9,5},... | collective-permute-start | bytes 589832 | tf_op jit(solution)/shard_map/ppermute | solution.py:48
  23.8 14.1 %collective-permute-start.10 = (bf16[2,16,3072]{2,1,0:T(8,128)(2,1)S(1)}, bf16[2,16,3072]{2,1,0:T(8,128)(2,1)S(1)}, u32[]{:S(2)}, u32[]{:S(2)}) collective-permute-start(bf16[2,16,3072]{2,1,0:T(8,128)(2,1)S(1)} %pad_maximum_fusion.1.refs_2_), channel_id=1, source_target_pairs={{0,1},{1,0},{2,3},{3,2},{4,5},{5,4},{6,7},{7,6},{8,9},{9,8},{10,11... | collective-permute-start | bytes 589832 | tf_op jit(solution)/shard_map/ppermute | solution.py:48
  27.2 12.6 %copy-start.10 = (bf16[2,16,3072]{2,1,0:T(8,128)(2,1)}, bf16[2,16,3072]{2,1,0:T(8,128)(2,1)S(1)}, u32[]{:S(2)}) copy-start(bf16[2,16,3072]{2,1,0:T(8,128)(2,1)S(1)} %collective-permute-done.5.refs_3_) | copy-start | bytes 589828
  27.2 12.5 %collective-permute-start.8 = (bf16[4,16,3072]{2,1,0:T(8,128)(2,1)S(1)}, bf16[4,16,3072]{2,1,0:T(8,128)(2,1)S(1)}, u32[]{:S(2)}, u32[]{:S(2)}) collective-permute-start(bf16[4,16,3072]{2,1,0:T(8,128)(2,1)S(1)} %pad_maximum_fusion.refs_0_), channel_id=1, source_target_pairs={{0,1},{1,0},{2,3},{3,2},{4,5},{5,4},{6,7},{7,6},{8,9},{9,8},{10,11... | collective-permute-start | bytes 1179656 | tf_op jit(solution)/shard_map/ppermute | solution.py:48
  27.2 12.6 %copy-start.7 = (bf16[4,16,3072]{2,1,0:T(8,128)(2,1)}, bf16[4,16,3072]{2,1,0:T(8,128)(2,1)S(1)}, u32[]{:S(2)}) copy-start(bf16[4,16,3072]{2,1,0:T(8,128)(2,1)S(1)} %collective-permute-done.3.refs_1_) | copy-start | bytes 1179652
  27.2 12.6 %collective-permute-start.9 = (bf16[4,16,3072]{2,1,0:T(8,128)(2,1)S(1)}, bf16[4,16,3072]{2,1,0:T(8,128)(2,1)S(1)}, u32[]{:S(2)}, u32[]{:S(2)}) collective-permute-start(bf16[4,16,3072]{2,1,0:T(8,128)(2,1)S(1)} %collective-permute-done.3.refs_1_), channel_id=1, source_target_pairs={{0,1},{1,0},{2,3},{3,2},{4,5},{5,4},{6,7},{7,6},{8,9},{9,8},{10,11... | collective-permute-start | bytes 1179656 | tf_op jit(solution)/shard_map/ppermute | solution.py:48
  37.4 2.5 copy-start.11
  37.4 2.4 collective-permute-start.11
  37.4 2.5 copy-start.12
  37.4 2.4 collective-permute-start.12
  37.9 2.0 copy-start.13
  37.9 1.9 collective-permute-start.13
  39.7 0.8 copy-start.8
  39.7 0.8 copy-start.15
  39.8 0.9 copy-start.16
  39.8 0.9 copy-start.17
  39.8 1.1 copy-start.9
  56.9 23.7 %all-to-all-start = ((bf16[16,6,16,256]{3,2,1,0:T(8,128)(2,1)}), bf16[16,6,16,256]{3,2,1,0:T(8,128)(2,1)S(1)}, u32[]{:S(2)}, u32[]{:S(2)}) async-start(bf16[16,6,16,256]{3,2,1,0:T(8,128)(2,1)} %bitcast.52), calls=%async_computation | async-start | bytes 1572864 | tf_op jit(solution)/shard_map/all_to_all | solution.py:418
  80.6 17.0 %copy-start.1 = (bf16[16,6,16,256]{3,2,1,0:T(8,128)(2,1)}, bf16[16,6,16,256]{3,2,1,0:T(8,128)(2,1)S(1)}, u32[]{:S(2)}) copy-start(bf16[16,6,16,256]{3,2,1,0:T(8,128)(2,1)S(1)} %all-to-all-done.x_ref) | copy-start | bytes 2359300
  80.6 24.2 %all-to-all-start.1 = ((bf16[16,6,16,256]{3,2,1,0:T(8,128)(2,1)}), bf16[16,6,16,256]{3,2,1,0:T(8,128)(2,1)S(1)}, u32[]{:S(2)}, u32[]{:S(2)}) async-start(bf16[16,6,16,256]{3,2,1,0:T(8,128)(2,1)} %bitcast.51), calls=%async_computation.1 | async-start | bytes 1572864 | tf_op jit(solution)/shard_map/all_to_all | solution.py:418
  86.1 24.2 %copy-start.18 = (f32[128]{0:T(128)S(1)}, f32[128]{0:T(128)}, u32[]{:S(2)}) copy-start(f32[128]{0:T(128)} %param.16) | copy-start | bytes 1540
  86.1 24.9 %copy-start.19 = (f32[128]{0:T(128)S(1)}, f32[128]{0:T(128)}, u32[]{:S(2)}) copy-start(f32[128]{0:T(128)} %param.17) | copy-start | bytes 1540
  104.8 18.4 %copy-start.2 = (bf16[16,6,16,256]{3,2,1,0:T(8,128)(2,1)}, bf16[16,6,16,256]{3,2,1,0:T(8,128)(2,1)S(1)}, u32[]{:S(2)}) copy-start(bf16[16,6,16,256]{3,2,1,0:T(8,128)(2,1)S(1)} %all-to-all-done.1.x_ref) | copy-start | bytes 2359300
  104.8 24.2 %all-to-all-start.2 = ((bf16[16,6,16,256]{3,2,1,0:T(8,128)(2,1)}), bf16[16,6,16,256]{3,2,1,0:T(8,128)(2,1)S(1)}, u32[]{:S(2)}, u32[]{:S(2)}) async-start(bf16[16,6,16,256]{3,2,1,0:T(8,128)(2,1)} %bitcast.50), calls=%async_computation.2 | async-start | bytes 1572864 | tf_op jit(solution)/shard_map/all_to_all | solution.py:418
  129.0 70.0 %copy-start.3 = (bf16[16,6,16,256]{3,2,1,0:T(8,128)(2,1)}, bf16[16,6,16,256]{3,2,1,0:T(8,128)(2,1)S(1)}, u32[]{:S(2)}) copy-start(bf16[16,6,16,256]{3,2,1,0:T(8,128)(2,1)S(1)} %all-to-all-done.2.x_ref) | copy-start | bytes 2359300
  129.0 79.3 %all-to-all-start.3 = ((bf16[16,6,16,256]{3,2,1,0:T(8,128)(2,1)}), bf16[16,6,16,256]{3,2,1,0:T(8,128)(2,1)S(1)}, u32[]{:S(2)}, u32[]{:S(2)}) async-start(bf16[16,6,16,256]{3,2,1,0:T(8,128)(2,1)} %bitcast.49), calls=%async_computation.3 | async-start | bytes 1572864 | tf_op jit(solution)/shard_map/all_to_all | solution.py:418
  208.3 0.9 copy-start.4
  213.8 22.6 %all-to-all-start.4 = ((f32[16,24,256]{2,1,0:T(8,128)}), f32[16,24,256]{2,1,0:T(8,128)S(1)}, u32[]{:S(2)}, u32[]{:S(2)}) async-start(f32[16,24,256]{2,1,0:T(8,128)} %broadcast_in_dim.4), calls=%async_computation.4 | async-start | bytes 786432 | tf_op jit(solution)/shard_map/all_to_all | solution.py:422
  236.5 2.6 copy-start.14
  242.9 15.0 %all-to-all-start.5 = ((f32[8,16,384]{2,0,1:T(8,128)}), f32[8,16,384]{2,0,1:T(8,128)S(1)}, u32[]{:S(2)}, u32[]{:S(2)}) async-start(f32[8,16,384]{2,0,1:T(8,128)} %bitcast.18), calls=%async_computation.5 | async-start | bytes 393216 | tf_op jit(solution)/shard_map/all_to_all | solution.py:440
  259.3 1.3 collective-permute-start.14
  260.9 4.3 %collective-permute-start.15 = (f32[9,1002]{1,0:T(8,128)S(1)}, f32[9,1002]{1,0:T(8,128)S(1)}, u32[]{:S(2)}, u32[]{:S(2)}) collective-permute-start(f32[9,1002]{1,0:T(8,128)S(1)} %select_maximum_fusion.2), channel_id=1, source_target_pairs={{0,2},{1,3},{2,0},{3,1},{4,6},{5,7},{6,4},{7,5},{8,10},{9,11},{10,... | collective-permute-start | bytes 108224 | tf_op jit(solution)/shard_map/ppermute | solution.py:48
  265.5 4.3 %collective-permute-start.16 = (f32[9,1002]{1,0:T(8,128)S(1)}, f32[9,1002]{1,0:T(8,128)S(1)}, u32[]{:S(2)}, u32[]{:S(2)}) collective-permute-start(f32[9,1002]{1,0:T(8,128)S(1)} %select_maximum_fusion.1), channel_id=1, source_target_pairs={{0,4},{1,5},{2,6},{3,7},{4,0},{5,1},{6,2},{7,3},{8,12},{9,13},{10,... | collective-permute-start | bytes 108224 | tf_op jit(solution)/shard_map/ppermute | solution.py:48
  270.1 5.4 %collective-permute-start.17 = (f32[9,1002]{1,0:T(8,128)S(1)}, f32[9,1002]{1,0:T(8,128)S(1)}, u32[]{:S(2)}, u32[]{:S(2)}) collective-permute-start(f32[9,1002]{1,0:T(8,128)S(1)} %select_maximum_fusion), channel_id=1, source_target_pairs={{0,8},{1,9},{2,10},{3,11},{4,12},{5,13},{6,14},{7,15},{8,0},{9,1},... | collective-permute-start | bytes 108224 | tf_op jit(solution)/shard_map/ppermute | solution.py:48
